TPU v7x, 128 devices: a whole 4x4x4 slice. The times are simulated.
128 devices in a mesh: grp: 64 (over z, y, x), dom: 2 (over core).
Axes of the slice: x: 4, y: 4, z: 4, core: 2. Of those that a mesh axis runs over, the one named last changes fastest.
Arguments:
- residual: float32 [64, 2048], P('grp', 'dom'), may hold values from -6 to 6
- op_blocks: float32 [64, 32, 64, 1728], P('grp', 'dom'), may hold values from -1 to 4
- block_cols: int32 [64, 32, 27], P('grp', 'dom'), may hold values from 0 to 47, as said below
- restrict_one: float32 [64, 64, 2048], P('grp', None, 'dom'), may hold values from -1 to 1
- restrict_two: float32 [64, 1024], P(None, 'dom'), may hold values from -1 to 1
- agg_one: int32 [16], replicated, may hold values from 0 to 15, each once
- agg_two: int32 [8], replicated, may hold values from 0 to 7, each once
Outputs:
- correction: float32 [64, 2048], P('grp', 'dom')
Inputs may be any that keep to these rules, and one draw needn't show every extreme that they name: `block_cols`: entry 0 of every row is the row's own block, 16 + (row index mod 16); an entry c names a block of the previous subdomain if c < 16, of the own one if c < 32, else of the next one; a row may name a block more than once. Each value once; block i belongs to aggregate agg_one[i] // 2. Each value once; level-two block m belongs to aggregate agg_two[m] // 2.
All inputs are finite; a program needn't handle non-finite values.
Results may differ from a plain program's by a relative error of at most 0.0003.
Values sent between devices are 32-bit elements; how exact they have to be, the bound alone decides.
A program may use at most 128 MiB of HBM per device.

v0:
```python
from functools import partial

import jax
import jax.numpy as jnp
from jax import lax
from jax.experimental import pallas as pl
from jax.experimental.pallas import tpu as pltpu
from jax.sharding import PartitionSpec as P

S2 = 3
S3 = 4
CENTER_VALUE = 2.3
HALF_WIDTH = 1.7
F32 = jnp.float32
BF16 = jnp.bfloat16
MESH = pl.DeviceIdType.MESH
A_CHUNKS = 4
PAIR = ((0, 1), (1, 0), (1, 1))
QUAD = PAIR + ((2, 0), (2, 1), (3, 0), (3, 1))
N_EX = 10


def pieces(value):
    hi = value.astype(BF16)
    lo = (value - hi.astype(F32)).astype(BF16)
    return hi, lo


def mm(a, b):
    return jnp.dot(a, b, preferred_element_type=F32)


def mm_nt(a, b):
    return lax.dot_general(a, b, (((1,), (1,)), ((), ())), preferred_element_type=F32)


def kernel(
    agg1_ref,
    agg2_ref,
    res_ref,
    cols_ref,
    r2_ref,
    r1_hbm,
    a_hbm,
    out_ref,
    a_buf,
    r1_buf,
    r31_buf,
    r2_blk,
    wp_ref,
    wr_ref,
    mask_ref,
    hot_ref,
    ug_ref,
    acc_ref,
    send_buf,
    recv_buf,
    a_sem,
    r1_sem,
    rx_send,
    rx_recv,
    send_sem,
    recv_sem,
):
    g = lax.axis_index("grp")
    d = lax.axis_index("dom")

    def peer(relation):
        bits, core = relation
        chip = g
        if bits & 1:
            chip = chip + 1 - 2 * (g % 2)
        if bits & 2:
            chip = chip + 2 - 4 * ((g // 2) % 2)
        return (chip, 1 - d if core else d)

    r1_copy = pltpu.make_async_copy(r1_hbm, r1_buf.at[pl.ds(d * 64, 64)], r1_sem)
    r1_copy.start()
    a_copies = []
    rows = 1024 // A_CHUNKS
    for part in range(A_CHUNKS):
        cut = pl.ds(part * rows, rows)
        a_copies.append(pltpu.make_async_copy(a_hbm.at[cut], a_buf.at[cut], a_sem.at[part]))
        a_copies[-1].start()

    barrier = pltpu.get_barrier_semaphore()
    for relation in QUAD:
        pl.semaphore_signal(barrier, inc=1, device_id=peer(relation), device_id_type=MESH)

    lane = lax.broadcasted_iota(jnp.int32, (8, 128), 1)
    row = lax.broadcasted_iota(jnp.int32, (8, 128), 0)
    left = lane < 64
    mine = (lane // 64) == d

    aggs = []
    for j in range(16):
        a = agg1_ref[j] // 2
        aggs.append(a)
    for jj in range(8):
        first, second = aggs[2 * jj], aggs[2 * jj + 1]
        m1 = jnp.where(left, first, second) == row
        m3 = jnp.where(left, agg2_ref[first] // 2, agg2_ref[second] // 2) == row
        cut = slice(jj * 128, (jj + 1) * 128)
        mask_ref[0, :, cut] = jnp.where(m1, 1.0, 0.0).astype(F32)
        mask_ref[1, :, cut] = jnp.where(m3, 1.0, 0.0).astype(F32)

    for m in range(8):
        r2_blk[m] = r2_ref[:, m * 64 : (m + 1) * 64]

    place = cols_ref[...] + 16 * (d - 1)
    valid = (place >= 0) & (place < 32)
    half = place % 2
    inner = (place // 16) * 8 + (place % 16) // 2
    even = jnp.where(valid, half * 16 + inner, -1)
    odd = jnp.where(valid, 32 + (1 - half) * 16 + inner, -1)
    spot = lax.broadcasted_iota(jnp.int32, (16, 128), 1) % 64
    for kk in range(14):
        hit = even[:, 2 * kk : 2 * kk + 1] == spot
        if 2 * kk + 1 < 27:
            hit = hit | (odd[:, 2 * kk + 1 : 2 * kk + 2] == spot)
        hot_ref[kk * 16 : (kk + 1) * 16, :] = jnp.where(hit, 1.0, 0.0).astype(BF16)

    def start_sends(ex, relations):
        copies = []
        for relation in relations:
            slot = QUAD.index(relation)
            copy = pltpu.make_async_remote_copy(
                src_ref=send_buf.at[ex],
                dst_ref=recv_buf.at[ex, slot],
                send_sem=send_sem.at[ex, slot],
                recv_sem=recv_sem.at[ex, slot],
                device_id=peer(relation),
                device_id_type=MESH,
            )
            copy.start()
            copies.append(copy)
        return copies

    started = []

    def own(value):
        return jnp.where(mine, value, 0.0)

    def send(ex, low, high, relations):
        send_buf[ex, 0:8] = own(low)
        if high is not None:
            send_buf[ex, 8:16] = own(high)
        copies = start_sends(ex, relations)
        started.extend(copies)
        return copies

    def total(ex, copies, relations, base, relations_used):
        slots = [QUAD.index(relation) for relation in relations_used]
        value = send_buf[ex, base : base + 8]
        for slot in slots:
            value = value + recv_buf[ex, slot, base : base + 8]
        return value

    def restrict(y):
        hi1, lo1 = pieces(y * mask_ref[0])
        hi3, lo3 = pieces(y * mask_ref[1])
        out = mm(jnp.concatenate([hi1, lo1, hi3, lo3], axis=0), wr_ref[...])
        s1 = out[0:8, 0:128] + out[8:16, 0:128]
        s3 = out[16:24, 128:256] + out[24:32, 128:256]
        return s1 + pltpu.roll(s1, 64, 1), s3 + pltpu.roll(s3, 64, 1)

    def prolong(v, level):
        v0 = jnp.where(left, v, 0.0)
        both = jnp.concatenate([v0, v - v0], axis=0)
        hi, lo = pieces(both)
        lhs = jnp.concatenate(
            [
                jnp.concatenate([hi, hi], axis=1),
                jnp.concatenate([lo, jnp.zeros_like(lo)], axis=1),
            ],
            axis=0,
        )
        prod = mm(lhs, wp_ref[level])
        prod = prod[0:16] + prod[16:32]
        rows_out = []
        for dd in range(2):
            for jj in range(8):
                cut = slice(jj * 128, (jj + 1) * 128)
                tile = prod[dd * 8 : dd * 8 + 8, cut] * mask_ref[level, :, cut]
                rows_out.append(jnp.sum(tile, axis=0, keepdims=True))
        return jnp.concatenate(rows_out, axis=0)

    def apply(v, level):
        u = prolong(v, level)
        turned = pltpu.roll(u, 64, 1)
        left16 = lax.broadcasted_iota(jnp.int32, (16, 128), 1) < 64
        spread = jnp.concatenate(
            [
                jnp.where(left16, u, 0.0),
                jnp.where(left16, turned, 0.0),
                jnp.where(left16, 0.0, u),
                jnp.where(left16, 0.0, turned),
            ],
            axis=0,
        )
        hi, lo = pieces(spread)
        gathered = mm(hot_ref[...], jnp.concatenate([hi, lo], axis=0))
        ug_ref[...] = gathered

        def block(i, carry):
            base = pl.multiple_of(i * 64, 64)
            acc = jnp.zeros((64, 128), F32)
            for kk in range(13):
                acc = acc + a_buf[pl.ds(base, 64), kk * 128 : (kk + 1) * 128] * ug_ref[
                    pl.ds(kk * 16 + i, 1), :
                ]
            tail = a_buf[pl.ds(base, 64), 1664:1728] * ug_ref[pl.ds(13 * 16 + i, 1), 0:64]
            acc = acc + jnp.concatenate([tail, jnp.zeros((64, 64), F32)], axis=1)
            acc_hi, acc_lo = pieces(acc)
            acc_ref[pl.ds(base, 64), 0:128] = acc_hi
            acc_ref[pl.ds(base, 64), 128:256] = acc_lo
            return carry

        lax.fori_loop(0, 16, block, 0, unroll=2)
        y = mm_nt(jnp.ones((16, 256), BF16), acc_ref[...])
        return restrict(y[0:8])

    r1_copy.wait()
    own_r1 = r1_buf[pl.ds(pl.multiple_of(d * 64, 64), 64), :]
    hi, lo = pieces(own_r1.T)
    wr_ref[:, 0:64] = hi
    wr_ref[:, 64:128] = lo
    wr_ref[:, 128:256] = jnp.zeros((1024, 128), BF16)

    pl.semaphore_wait(barrier, len(QUAD))

    def swap_copy(buf, index):
        ref = buf.at[pl.ds(d * 64, 64)]
        return pltpu.make_async_remote_copy(
            src_ref=ref,
            dst_ref=ref,
            send_sem=rx_send.at[index],
            recv_sem=rx_recv.at[index],
            device_id=(g, 1 - d),
            device_id_type=MESH,
        )

    swap1 = swap_copy(r1_buf, 0)
    swap1.start()

    y0 = jnp.broadcast_to(res_ref[...], (8, 1024))
    w, unused = restrict(y0)
    copies = send(0, w, None, PAIR)

    for jj in range(8):
        parts = []
        for half_at in range(2):
            j = 2 * jj + half_at
            parts.append(
                jnp.dot(
                    r2_blk[aggs[j]],
                    own_r1[:, j * 64 : (j + 1) * 64],
                    preferred_element_type=F32,
                    precision=lax.Precision.HIGHEST,
                )
            )
        r31_buf[pl.ds(pl.multiple_of(d * 64, 64), 64), jj * 128 : (jj + 1) * 128] = jnp.concatenate(
            parts, axis=1
        )
    own_r31 = r31_buf[pl.ds(pl.multiple_of(d * 64, 64), 64), :]
    swap3 = swap_copy(r31_buf, 1)
    swap3.start()
    hi, lo = pieces(own_r31.T)
    wr_ref[:, 128:192] = hi
    wr_ref[:, 192:256] = lo
    unused, coarse = restrict(y0)

    swap1.wait()
    hi, lo = pieces(r1_buf[...])
    wp_ref[0, 0:128] = hi
    wp_ref[0, 128:256] = lo

    for copy in a_copies:
        copy.wait()

    spread_ratio = CENTER_VALUE / HALF_WIDTH

    def wait_all(copies):
        for copy in copies:
            copy.wait_recv()

    def pair_total(ex, copies):
        wait_all(copies)
        return total(ex, copies, PAIR, 0, PAIR)

    def quad_total(ex, copies, base=0):
        wait_all(copies)
        return total(ex, copies, QUAD, base, QUAD)

    rest = pair_total(0, copies)
    start = jnp.zeros((8, 128), F32)
    direction = rest / CENTER_VALUE
    ratio = 1.0 / spread_ratio
    for sweep in range(S2):
        ex = 1 + sweep
        start = start + direction
        w, w3 = apply(direction, 0)
        coarse = coarse - w3
        if sweep == S2 - 1:
            copies = send(ex, w, coarse, QUAD)
            if True:
                swap3.wait()
                hi, lo = pieces(r31_buf[...])
                wp_ref[1, 0:128] = hi
                wp_ref[1, 128:256] = lo
            wait_all(copies)
            rest = rest - total(ex, copies, QUAD, 0, PAIR)
            rhs3 = total(ex, copies, QUAD, 8, QUAD)
        else:
            copies = send(ex, w, None, PAIR)
            rest = rest - pair_total(ex, copies)
            ratio_next = 1.0 / (2.0 * spread_ratio - ratio)
            direction = ratio_next * ratio * direction + 2.0 * ratio_next / HALF_WIDTH * rest
            ratio = ratio_next

    rest3 = rhs3
    coarse_sol = jnp.zeros((8, 128), F32)
    direction = rest3 / CENTER_VALUE
    ratio = 1.0 / spread_ratio
    for sweep in range(S3):
        coarse_sol = coarse_sol + direction
        if sweep < S3 - 1:
            ex = 1 + S2 + sweep
            unused, w3 = apply(direction, 1)
            copies = send(ex, w3, None, QUAD)
            rest3 = rest3 - quad_total(ex, copies)
            ratio_next = 1.0 / (2.0 * spread_ratio - ratio)
            direction = ratio_next * ratio * direction + 2.0 * ratio_next / HALF_WIDTH * rest3
            ratio = ratio_next

    ex = S2 + S3
    w, unused = apply(coarse_sol, 1)
    copies = send(ex, w, None, PAIR)
    rest = rest - pair_total(ex, copies)
    direction = rest / CENTER_VALUE
    ratio = 1.0 / spread_ratio
    for sweep in range(S2):
        start = start + direction
        if sweep < S2 - 1:
            ex = S2 + S3 + 1 + sweep
            w, unused = apply(direction, 0)
            copies = send(ex, w, None, PAIR)
            rest = rest - pair_total(ex, copies)
            ratio_next = 1.0 / (2.0 * spread_ratio - ratio)
            direction = ratio_next * ratio * direction + 2.0 * ratio_next / HALF_WIDTH * rest
            ratio = ratio_next

    fine = prolong(start, 0) + prolong(coarse_sol, 1)
    out_ref[...] = jnp.where(d == 0, fine[0:8], fine[8:16])

    swap_done = [copy.wait_send() for copy in started]


def body(residual, op_blocks, block_cols, restrict_one, restrict_two, agg_one, agg_two):
    vmem = pl.BlockSpec(memory_space=pltpu.VMEM)
    smem = pl.BlockSpec(memory_space=pltpu.SMEM)
    anywhere = pl.BlockSpec(memory_space=pl.ANY)
    out = pl.pallas_call(
        kernel,
        out_shape=jax.ShapeDtypeStruct((8, 128), F32),
        in_specs=[smem, smem, vmem, vmem, vmem, anywhere, anywhere],
        out_specs=vmem,
        scratch_shapes=[
            pltpu.VMEM((1024, 1728), F32),
            pltpu.VMEM((128, 1024), F32),
            pltpu.VMEM((128, 1024), F32),
            pltpu.VMEM((8, 64, 64), F32),
            pltpu.VMEM((2, 256, 1024), BF16),
            pltpu.VMEM((1024, 256), BF16),
            pltpu.VMEM((2, 8, 1024), F32),
            pltpu.VMEM((224, 128), BF16),
            pltpu.VMEM((224, 128), F32),
            pltpu.VMEM((1024, 256), BF16),
            pltpu.VMEM((N_EX, 16, 128), F32),
            pltpu.VMEM((N_EX, len(QUAD), 16, 128), F32),
            pltpu.SemaphoreType.DMA((A_CHUNKS,)),
            pltpu.SemaphoreType.DMA,
            pltpu.SemaphoreType.DMA((2,)),
            pltpu.SemaphoreType.DMA((2,)),
            pltpu.SemaphoreType.DMA((N_EX, len(QUAD))),
            pltpu.SemaphoreType.DMA((N_EX, len(QUAD))),
        ],
        compiler_params=pltpu.CompilerParams(
            collective_id=0, has_side_effects=True, vmem_limit_bytes=48 * 1024 * 1024
        ),
        cost_estimate=pl.CostEstimate(
            flops=40_000_000, bytes_accessed=7_500_000, transcendentals=0
        ),
    )(
        agg_one,
        agg_two,
        residual,
        block_cols[0],
        restrict_two,
        restrict_one[0],
        op_blocks.reshape(1024, 1728),
    )
    return out.reshape(1, 1024)


def solution(mesh):
    placed = (
        P("grp", "dom"),
        P("grp", "dom", None, None),
        P("grp", "dom", None),
        P("grp", None, "dom"),
        P(None, "dom"),
        P(),
        P(),
    )
    return jax.shard_map(
        body, mesh=mesh, in_specs=placed, out_specs=P("grp", "dom"), check_vma=False
    )
```

profile of v0, /device:TPU:1, one launch (start us, length us, event | category | flops | bytes accessed | tf_op | source)
XLA Modules:
  0.0 57.0 jit_solution(79855685640453939)
XLA Ops:
  0.0 0.0 copy-start
  0.0 0.9 %copy-done = f32[1,64,1024]{2,1,0:T(8,128)S(1)} copy-done((f32[1,64,1024]{2,1,0:T(8,128)S(1)}, f32[1,64,1024]{2,1,0:T(8,128)}, u32[]{:S(2)}) %copy-start) | copy-done | bytes 262168
  1.0 0.0 copy-start.1
  1.0 0.9 %copy-done.1 = f32[64,512]{1,0:T(8,128)S(1)} copy-done((f32[64,512]{1,0:T(8,128)S(1)}, f32[64,512]{1,0:T(8,128)}, u32[]{:S(2)}) %copy-start.1) | copy-done | bytes 131096
  1.9 0.0 copy-start.2
  1.9 0.7 %copy-done.2 = s32[1,16,27]{2,1,0:T(8,128)S(1)} copy-done((s32[1,16,27]{2,1,0:T(8,128)S(1)}, s32[1,16,27]{2,1,0:T(8,128)}, u32[]{:S(2)}) %copy-start.2) | copy-done | bytes 1752
  2.6 0.0 copy-start.3
  2.6 0.7 %copy-done.3 = f32[1,1024]{1,0:T(1,128)S(1)} copy-done((f32[1,1024]{1,0:T(1,128)S(1)}, f32[1,1024]{1,0:T(1,128)}, u32[]{:S(2)}) %copy-start.3) | copy-done | bytes 4120
  3.2 0.0 copy-start.4
  3.2 0.7 %copy-done.4 = s32[16]{0:T(128)S(1)} copy-done((s32[16]{0:T(128)S(1)}, s32[16]{0:T(128)}, u32[]{:S(2)}) %copy-start.4) | copy-done | bytes 88
  3.9 0.0 copy-start.5
  3.9 0.7 %copy-done.5 = s32[8]{0:T(128)S(1)} copy-done((s32[8]{0:T(128)S(1)}, s32[8]{0:T(128)}, u32[]{:S(2)}) %copy-start.5) | copy-done | bytes 56
  4.6 51.9 %shard_map.73 = f32[8,128]{1,0:T(8,128)S(1)} custom-call(s32[16]{0:T(128)S(1)} %copy-done.4, s32[8]{0:T(128)S(1)} %copy-done.5, f32[1,1024]{1,0:T(1,128)S(1)} %copy-done.3, s32[16,27]{1,0:T(8,128)S(1)} %bitcast.6, f32[64,512]{1,0:T(8,128)S(1)} %copy-done.1, f32[64,1024]{1,0:T(8,128)S(1)} %bitcast.4, f32[1024,1728]{1,0:T(8,128)} %bitcast.7), custom_call_target="tpu_custom_call" | custom-call | flops 40000000 | bytes 7500000 | tf_op jit(solution)/shard_map/pallas_call | solution.py:363
  56.4 0.6 %copy.9 = f32[1,1024]{1,0:T(1,128)} copy(f32[1,1024]{1,0:T(1,128)S(1)} %bitcast.5) | data formatting | bytes 8192
Async XLA Ops:
  0.0 0.9 %copy-start = (f32[1,64,1024]{2,1,0:T(8,128)S(1)}, f32[1,64,1024]{2,1,0:T(8,128)}, u32[]{:S(2)}) copy-start(f32[1,64,1024]{2,1,0:T(8,128)} %param.10) | copy-start | bytes 786436
  1.0 0.9 %copy-start.1 = (f32[64,512]{1,0:T(8,128)S(1)}, f32[64,512]{1,0:T(8,128)}, u32[]{:S(2)}) copy-start(f32[64,512]{1,0:T(8,128)} %r2_ref.1) | copy-start | bytes 393220
  1.9 0.7 %copy-start.2 = (s32[1,16,27]{2,1,0:T(8,128)S(1)}, s32[1,16,27]{2,1,0:T(8,128)}, u32[]{:S(2)}) copy-start(s32[1,16,27]{2,1,0:T(8,128)} %param.9) | copy-start | bytes 5188
  2.6 0.7 %copy-start.3 = (f32[1,1024]{1,0:T(1,128)S(1)}, f32[1,1024]{1,0:T(1,128)}, u32[]{:S(2)}) copy-start(f32[1,1024]{1,0:T(1,128)} %res_ref.1) | copy-start | bytes 12292
  3.2 0.7 %copy-start.4 = (s32[16]{0:T(128)S(1)}, s32[16]{0:T(128)}, u32[]{:S(2)}) copy-start(s32[16]{0:T(128)} %agg1_ref.1) | copy-start | bytes 196
  3.9 0.7 %copy-start.5 = (s32[8]{0:T(128)S(1)}, s32[8]{0:T(128)}, u32[]{:S(2)}) copy-start(s32[8]{0:T(128)} %agg2_ref.1) | copy-start | bytes 100
where the time goes:
time: 57.2 us; the launch traced here: 57 us
  Pallas kernels  51.9 us (91%)
  local copies, waits for them, and re-layouts  5.14 us (9%)
    pallas_call x1, Pallas kernels, body(): pl.pallas_call(kernel, out_shape=jax.ShapeDtypeStruct((8, 128), F32), in_...  51.9 us
    unnamed x13, local copies, waits for them, and re-layouts  5.14 us

commit v1 on v0

--- a/solution.py
+++ b/solution.py
@@ -15,8 +15,8 @@
 BF16 = jnp.bfloat16
 MESH = pl.DeviceIdType.MESH
 A_CHUNKS = 4
-PAIR = ((0, 1), (1, 0), (1, 1))
-QUAD = PAIR + ((2, 0), (2, 1), (3, 0), (3, 1))
+PAIR = ((1, 0), (1, 1), (0, 1))
+QUAD = ((2, 0), (3, 0), (2, 1), (3, 1)) + PAIR
 N_EX = 10
 
 
@@ -35,14 +35,19 @@
 
 
 def kernel(
+    agg1_hbm,
+    agg2_hbm,
+    res_hbm,
+    cols_hbm,
+    r2_hbm,
+    r1_hbm,
+    a_hbm,
+    out_ref,
     agg1_ref,
     agg2_ref,
     res_ref,
     cols_ref,
     r2_ref,
-    r1_hbm,
-    a_hbm,
-    out_ref,
     a_buf,
     r1_buf,
     r31_buf,
@@ -50,13 +55,12 @@
     wp_ref,
     wr_ref,
     mask_ref,
-    hot_ref,
-    ug_ref,
-    acc_ref,
+    table_ref,
     send_buf,
     recv_buf,
     a_sem,
     r1_sem,
+    in_sem,
     rx_send,
     rx_recv,
     send_sem,
@@ -76,6 +80,18 @@
 
     r1_copy = pltpu.make_async_copy(r1_hbm, r1_buf.at[pl.ds(d * 64, 64)], r1_sem)
     r1_copy.start()
+    inputs = []
+    for index, (source, target) in enumerate(
+        (
+            (agg1_hbm, agg1_ref),
+            (agg2_hbm, agg2_ref),
+            (cols_hbm, cols_ref),
+            (res_hbm, res_ref),
+            (r2_hbm, r2_ref),
+        )
+    ):
+        inputs.append(pltpu.make_async_copy(source, target, in_sem.at[index]))
+        inputs[-1].start()
     a_copies = []
     rows = 1024 // A_CHUNKS
     for part in range(A_CHUNKS):
@@ -91,6 +107,9 @@
     row = lax.broadcasted_iota(jnp.int32, (8, 128), 0)
     left = lane < 64
     mine = (lane // 64) == d
+
+    for copy in inputs:
+        copy.wait()
 
     aggs = []
     for j in range(16):
@@ -107,18 +126,9 @@
     for m in range(8):
         r2_blk[m] = r2_ref[:, m * 64 : (m + 1) * 64]
 
-    place = cols_ref[...] + 16 * (d - 1)
-    valid = (place >= 0) & (place < 32)
-    half = place % 2
-    inner = (place // 16) * 8 + (place % 16) // 2
-    even = jnp.where(valid, half * 16 + inner, -1)
-    odd = jnp.where(valid, 32 + (1 - half) * 16 + inner, -1)
-    spot = lax.broadcasted_iota(jnp.int32, (16, 128), 1) % 64
-    for kk in range(14):
-        hit = even[:, 2 * kk : 2 * kk + 1] == spot
-        if 2 * kk + 1 < 27:
-            hit = hit | (odd[:, 2 * kk + 1 : 2 * kk + 2] == spot)
-        hot_ref[kk * 16 : (kk + 1) * 16, :] = jnp.where(hit, 1.0, 0.0).astype(BF16)
+    for entry in range(16):
+        table_ref[0, 32 * d + entry] = jnp.zeros((8, 128), F32)
+        table_ref[1, 32 * d + entry] = jnp.zeros((8, 128), F32)
 
     def start_sends(ex, relations):
         copies = []
@@ -156,13 +166,19 @@
             value = value + recv_buf[ex, slot, base : base + 8]
         return value
 
-    def restrict(y):
-        hi1, lo1 = pieces(y * mask_ref[0])
-        hi3, lo3 = pieces(y * mask_ref[1])
-        out = mm(jnp.concatenate([hi1, lo1, hi3, lo3], axis=0), wr_ref[...])
+    def restrict_part(y, group, rows):
+        cut = slice(group * rows, (group + 1) * rows)
+        hi1, lo1 = pieces(y * mask_ref[0, :, cut])
+        hi3, lo3 = pieces(y * mask_ref[1, :, cut])
+        return mm(jnp.concatenate([hi1, lo1, hi3, lo3], axis=0), wr_ref[cut])
+
+    def restrict_end(out):
         s1 = out[0:8, 0:128] + out[8:16, 0:128]
         s3 = out[16:24, 128:256] + out[24:32, 128:256]
         return s1 + pltpu.roll(s1, 64, 1), s3 + pltpu.roll(s3, 64, 1)
+
+    def restrict(y):
+        return restrict_end(restrict_part(y, 0, 1024))
 
     def prolong(v, level):
         v0 = jnp.where(left, v, 0.0)
@@ -175,50 +191,59 @@
             ],
             axis=0,
         )
-        prod = mm(lhs, wp_ref[level])
-        prod = prod[0:16] + prod[16:32]
-        rows_out = []
+        tiles = [[], []]
+        for quarter in range(4):
+            prod = mm(lhs, wp_ref[level, :, quarter * 256 : (quarter + 1) * 256])
+            prod = prod[0:16] + prod[16:32]
+            for dd in range(2):
+                for part in range(2):
+                    jj = 2 * quarter + part
+                    tile = prod[dd * 8 : dd * 8 + 8, part * 128 : (part + 1) * 128]
+                    tile = tile * mask_ref[level, :, jj * 128 : (jj + 1) * 128]
+                    tile = tile + pltpu.roll(tile, 4, 0)
+                    tile = tile + pltpu.roll(tile, 2, 0)
+                    tile = tile + pltpu.roll(tile, 1, 0)
+                    tiles[dd].append(tile)
+        return tiles
+
+    def own_rows(tiles):
+        value = jnp.zeros((8, 128), F32)
+        for jj in range(8):
+            value = jnp.where(row == jj, jnp.where(d == 0, tiles[0][jj], tiles[1][jj]), value)
+        return value
+
+    def apply(v, level):
+        tiles = prolong(v, level)
         for dd in range(2):
+            base = (dd - d + 1) * 16
             for jj in range(8):
-                cut = slice(jj * 128, (jj + 1) * 128)
-                tile = prod[dd * 8 : dd * 8 + 8, cut] * mask_ref[level, :, cut]
-                rows_out.append(jnp.sum(tile, axis=0, keepdims=True))
-        return jnp.concatenate(rows_out, axis=0)
-
-    def apply(v, level):
-        u = prolong(v, level)
-        turned = pltpu.roll(u, 64, 1)
-        left16 = lax.broadcasted_iota(jnp.int32, (16, 128), 1) < 64
-        spread = jnp.concatenate(
-            [
-                jnp.where(left16, u, 0.0),
-                jnp.where(left16, turned, 0.0),
-                jnp.where(left16, 0.0, u),
-                jnp.where(left16, 0.0, turned),
-            ],
-            axis=0,
-        )
-        hi, lo = pieces(spread)
-        gathered = mm(hot_ref[...], jnp.concatenate([hi, lo], axis=0))
-        ug_ref[...] = gathered
-
-        def block(i, carry):
-            base = pl.multiple_of(i * 64, 64)
-            acc = jnp.zeros((64, 128), F32)
-            for kk in range(13):
-                acc = acc + a_buf[pl.ds(base, 64), kk * 128 : (kk + 1) * 128] * ug_ref[
-                    pl.ds(kk * 16 + i, 1), :
-                ]
-            tail = a_buf[pl.ds(base, 64), 1664:1728] * ug_ref[pl.ds(13 * 16 + i, 1), 0:64]
-            acc = acc + jnp.concatenate([tail, jnp.zeros((64, 64), F32)], axis=1)
-            acc_hi, acc_lo = pieces(acc)
-            acc_ref[pl.ds(base, 64), 0:128] = acc_hi
-            acc_ref[pl.ds(base, 64), 128:256] = acc_lo
-            return carry
-
-        lax.fori_loop(0, 16, block, 0, unroll=2)
-        y = mm_nt(jnp.ones((16, 256), BF16), acc_ref[...])
-        return restrict(y[0:8])
+                tile = tiles[dd][jj]
+                turned = pltpu.roll(tile, 64, 1)
+                table_ref[0, base + 2 * jj] = tile
+                table_ref[1, base + 2 * jj + 1] = tile
+                table_ref[0, base + 2 * jj + 1] = turned
+                table_ref[1, base + 2 * jj] = turned
+        out = None
+        for group in range(4):
+            sums = []
+            for i in range(group * 4, group * 4 + 4):
+                base = i * 64
+                acc = jnp.zeros((8, 8, 128), F32)
+                for kk in range(13):
+                    u = jnp.where(
+                        left, table_ref[0, cols_ref[i, 2 * kk]], table_ref[1, cols_ref[i, 2 * kk + 1]]
+                    )
+                    block = a_buf[base : base + 64, kk * 128 : (kk + 1) * 128]
+                    acc = acc + block.reshape(8, 8, 128) * u[None]
+                u = table_ref[0, cols_ref[i, 26]]
+                tail = a_buf[base : base + 64, 1664:1728].reshape(8, 8, 64) * u[None, :, 0:64]
+                acc = acc + jnp.concatenate([tail, jnp.zeros((8, 8, 64), F32)], axis=2)
+                acc_hi, acc_lo = pieces(acc.reshape(64, 128))
+                sums.append(jnp.concatenate([acc_hi, acc_lo], axis=1))
+            y = mm_nt(jnp.ones((16, 256), BF16), jnp.concatenate(sums, axis=0))
+            part = restrict_part(y[0:8], group, 256)
+            out = part if out is None else out + part
+        return restrict_end(out)
 
     r1_copy.wait()
     own_r1 = r1_buf[pl.ds(pl.multiple_of(d * 64, 64), 64), :]
@@ -303,11 +328,10 @@
         coarse = coarse - w3
         if sweep == S2 - 1:
             copies = send(ex, w, coarse, QUAD)
-            if True:
-                swap3.wait()
-                hi, lo = pieces(r31_buf[...])
-                wp_ref[1, 0:128] = hi
-                wp_ref[1, 128:256] = lo
+            swap3.wait()
+            hi, lo = pieces(r31_buf[...])
+            wp_ref[1, 0:128] = hi
+            wp_ref[1, 128:256] = lo
             wait_all(copies)
             rest = rest - total(ex, copies, QUAD, 0, PAIR)
             rhs3 = total(ex, copies, QUAD, 8, QUAD)
@@ -336,6 +360,7 @@
     ex = S2 + S3
     w, unused = apply(coarse_sol, 1)
     copies = send(ex, w, None, PAIR)
+    fine_coarse = own_rows(prolong(coarse_sol, 1))
     rest = rest - pair_total(ex, copies)
     direction = rest / CENTER_VALUE
     ratio = 1.0 / spread_ratio
@@ -350,22 +375,26 @@
             direction = ratio_next * ratio * direction + 2.0 * ratio_next / HALF_WIDTH * rest
             ratio = ratio_next
 
-    fine = prolong(start, 0) + prolong(coarse_sol, 1)
-    out_ref[...] = jnp.where(d == 0, fine[0:8], fine[8:16])
-
-    swap_done = [copy.wait_send() for copy in started]
+    out_ref[...] = own_rows(prolong(start, 0)) + fine_coarse
+
+    for copy in started:
+        copy.wait_send()
 
 
 def body(residual, op_blocks, block_cols, restrict_one, restrict_two, agg_one, agg_two):
     vmem = pl.BlockSpec(memory_space=pltpu.VMEM)
-    smem = pl.BlockSpec(memory_space=pltpu.SMEM)
-    anywhere = pl.BlockSpec(memory_space=pl.ANY)
+    hbm = pl.BlockSpec(memory_space=pltpu.HBM)
     out = pl.pallas_call(
         kernel,
         out_shape=jax.ShapeDtypeStruct((8, 128), F32),
-        in_specs=[smem, smem, vmem, vmem, vmem, anywhere, anywhere],
+        in_specs=[hbm] * 7,
         out_specs=vmem,
         scratch_shapes=[
+            pltpu.SMEM((16,), jnp.int32),
+            pltpu.SMEM((8,), jnp.int32),
+            pltpu.VMEM((1, 1024), F32),
+            pltpu.SMEM((16, 27), jnp.int32),
+            pltpu.VMEM((64, 512), F32),
             pltpu.VMEM((1024, 1728), F32),
             pltpu.VMEM((128, 1024), F32),
             pltpu.VMEM((128, 1024), F32),
@@ -373,13 +402,12 @@
             pltpu.VMEM((2, 256, 1024), BF16),
             pltpu.VMEM((1024, 256), BF16),
             pltpu.VMEM((2, 8, 1024), F32),
-            pltpu.VMEM((224, 128), BF16),
-            pltpu.VMEM((224, 128), F32),
-            pltpu.VMEM((1024, 256), BF16),
+            pltpu.VMEM((2, 48, 8, 128), F32),
             pltpu.VMEM((N_EX, 16, 128), F32),
             pltpu.VMEM((N_EX, len(QUAD), 16, 128), F32),
             pltpu.SemaphoreType.DMA((A_CHUNKS,)),
             pltpu.SemaphoreType.DMA,
+            pltpu.SemaphoreType.DMA((5,)),
             pltpu.SemaphoreType.DMA((2,)),
             pltpu.SemaphoreType.DMA((2,)),
             pltpu.SemaphoreType.DMA((N_EX, len(QUAD))),
@@ -392,13 +420,18 @@
             flops=40_000_000, bytes_accessed=7_500_000, transcendentals=0
         ),
     )(
-        agg_one,
-        agg_two,
-        residual,
-        block_cols[0],
-        restrict_two,
-        restrict_one[0],
-        op_blocks.reshape(1024, 1728),
+        *(
+            pltpu.with_memory_space_constraint(value, pltpu.HBM)
+            for value in (
+                agg_one,
+                agg_two,
+                residual,
+                block_cols[0],
+                restrict_two,
+                restrict_one[0],
+                op_blocks.reshape(1024, 1728),
+            )
+        )
     )
     return out.reshape(1, 1024)
 

time: 57.2 us -> 48.7 us (0.85)
  local copies, waits for them, and re-layouts: 5.14 us -> 0.6 us
  Pallas kernels: 51.9 us -> 48 us
    unnamed x13 -> x1, local copies, waits for them, and re-layouts: 5.14 us -> 0.6 us
    pallas_call x1, Pallas kernels: 51.9 us -> 48 us  [body(): pl.pallas_call(kernel, out_shape=jax.ShapeDtypeStruct((8, 128), F32), in_...]
where the time goes in v1:
time: 48.7 us; the launch traced here: 48.6 us
  Pallas kernels  48 us (99%)
  local copies, waits for them, and re-layouts  0.6 us (1%)
    pallas_call x1, Pallas kernels, body(): pl.pallas_call(kernel, out_shape=jax.ShapeDtypeStruct((8, 128), F32), in_...  48 us

profile of v1, /device:TPU:1, one launch (start us, length us, event | category | flops | bytes accessed | tf_op | source)
XLA Modules:
  0.0 48.6 jit_solution(10545610013716549796)
XLA Ops:
  0.0 48.0 %shard_map.73 = f32[8,128]{1,0:T(8,128)S(1)} custom-call(s32[16]{0:T(128)} %agg1_hbm.1, s32[8]{0:T(128)} %agg2_hbm.1, f32[1,1024]{1,0:T(1,128)} %res_hbm.1, s32[16,27]{1,0:T(8,128)} %bitcast.7, f32[64,512]{1,0:T(8,128)} %r2_hbm.1, f32[64,1024]{1,0:T(8,128)} %bitcast.6, f32[1024,1728]{1,0:T(8,128)} %bitcast.5), custom_call_target="tpu_custom_call" | custom-call | flops 40000000 | bytes 7500000 | tf_op jit(solution)/shard_map/pallas_call | solution.py:387
  48.0 0.6 %copy.9 = f32[1,1024]{1,0:T(1,128)} copy(f32[1,1024]{1,0:T(1,128)S(1)} %bitcast.4) | data formatting | bytes 8192

commit v2 on v1

--- a/solution.py
+++ b/solution.py
@@ -28,10 +28,6 @@
 
 def mm(a, b):
     return jnp.dot(a, b, preferred_element_type=F32)
-
-
-def mm_nt(a, b):
-    return lax.dot_general(a, b, (((1,), (1,)), ((), ())), preferred_element_type=F32)
 
 
 def kernel(
@@ -55,7 +51,10 @@
     wp_ref,
     wr_ref,
     mask_ref,
-    table_ref,
+    hot_ref,
+    ug_ref,
+    rt_ref,
+    pick_ref,
     send_buf,
     recv_buf,
     a_sem,
@@ -123,20 +122,32 @@
         mask_ref[0, :, cut] = jnp.where(m1, 1.0, 0.0).astype(F32)
         mask_ref[1, :, cut] = jnp.where(m3, 1.0, 0.0).astype(F32)
 
+    for j in range(16):
+        pick_ref[j] = jnp.where(jnp.where(left, aggs[j], agg2_ref[aggs[j]] // 2) == row, 1.0, 0.0)
+
     for m in range(8):
         r2_blk[m] = r2_ref[:, m * 64 : (m + 1) * 64]
 
-    for entry in range(16):
-        table_ref[0, 32 * d + entry] = jnp.zeros((8, 128), F32)
-        table_ref[1, 32 * d + entry] = jnp.zeros((8, 128), F32)
-
-    def start_sends(ex, relations):
+    place = cols_ref[...] + 16 * (d - 1)
+    valid = (place >= 0) & (place < 32)
+    half = place % 2
+    inner = (place // 16) * 8 + (place % 16) // 2
+    even = jnp.where(valid, half * 16 + inner, -1)
+    odd = jnp.where(valid, 32 + (1 - half) * 16 + inner, -1)
+    spot = lax.broadcasted_iota(jnp.int32, (16, 128), 1) % 64
+    for kk in range(14):
+        hit = even[:, 2 * kk : 2 * kk + 1] == spot
+        if 2 * kk + 1 < 27:
+            hit = hit | (odd[:, 2 * kk + 1 : 2 * kk + 2] == spot)
+        hot_ref[kk * 16 : (kk + 1) * 16, :] = jnp.where(hit, 1.0, 0.0).astype(BF16)
+
+    def start_sends(ex, relations, rows):
         copies = []
         for relation in relations:
             slot = QUAD.index(relation)
             copy = pltpu.make_async_remote_copy(
-                src_ref=send_buf.at[ex],
-                dst_ref=recv_buf.at[ex, slot],
+                src_ref=send_buf.at[ex, 0:rows],
+                dst_ref=recv_buf.at[ex, slot, 0:rows],
                 send_sem=send_sem.at[ex, slot],
                 recv_sem=recv_sem.at[ex, slot],
                 device_id=peer(relation),
@@ -155,7 +166,7 @@
         send_buf[ex, 0:8] = own(low)
         if high is not None:
             send_buf[ex, 8:16] = own(high)
-        copies = start_sends(ex, relations)
+        copies = start_sends(ex, relations, 8 if high is None else 16)
         started.extend(copies)
         return copies
 
@@ -206,48 +217,55 @@
                     tiles[dd].append(tile)
         return tiles
 
+    def rows_of(tiles):
+        value = tiles[0]
+        for jj in range(1, 8):
+            value = jnp.where(row == jj, tiles[jj], value)
+        return value
+
     def own_rows(tiles):
-        value = jnp.zeros((8, 128), F32)
-        for jj in range(8):
-            value = jnp.where(row == jj, jnp.where(d == 0, tiles[0][jj], tiles[1][jj]), value)
-        return value
+        return jnp.where(d == 0, rows_of(tiles[0]), rows_of(tiles[1]))
 
     def apply(v, level):
         tiles = prolong(v, level)
-        for dd in range(2):
-            base = (dd - d + 1) * 16
-            for jj in range(8):
-                tile = tiles[dd][jj]
-                turned = pltpu.roll(tile, 64, 1)
-                table_ref[0, base + 2 * jj] = tile
-                table_ref[1, base + 2 * jj + 1] = tile
-                table_ref[0, base + 2 * jj + 1] = turned
-                table_ref[1, base + 2 * jj] = turned
+        u = jnp.concatenate([rows_of(tiles[0]), rows_of(tiles[1])], axis=0)
+        turned = pltpu.roll(u, 64, 1)
+        left16 = jnp.concatenate([left, left], axis=0)
+        spread = jnp.concatenate(
+            [
+                jnp.where(left16, u, 0.0),
+                jnp.where(left16, turned, 0.0),
+                jnp.where(left16, 0.0, u),
+                jnp.where(left16, 0.0, turned),
+            ],
+            axis=0,
+        )
+        hi, lo = pieces(spread)
+        ug_ref[...] = mm(hot_ref[...], jnp.concatenate([hi, lo], axis=0))
         out = None
-        for group in range(4):
-            sums = []
-            for i in range(group * 4, group * 4 + 4):
-                base = i * 64
-                acc = jnp.zeros((8, 8, 128), F32)
-                for kk in range(13):
-                    u = jnp.where(
-                        left, table_ref[0, cols_ref[i, 2 * kk]], table_ref[1, cols_ref[i, 2 * kk + 1]]
-                    )
-                    block = a_buf[base : base + 64, kk * 128 : (kk + 1) * 128]
-                    acc = acc + block.reshape(8, 8, 128) * u[None]
-                u = table_ref[0, cols_ref[i, 26]]
-                tail = a_buf[base : base + 64, 1664:1728].reshape(8, 8, 64) * u[None, :, 0:64]
-                acc = acc + jnp.concatenate([tail, jnp.zeros((8, 8, 64), F32)], axis=2)
-                acc_hi, acc_lo = pieces(acc.reshape(64, 128))
-                sums.append(jnp.concatenate([acc_hi, acc_lo], axis=1))
-            y = mm_nt(jnp.ones((16, 256), BF16), jnp.concatenate(sums, axis=0))
-            part = restrict_part(y[0:8], group, 256)
+        for i in range(16):
+            base = i * 64
+            acc = jnp.zeros((8, 8, 128), F32)
+            for kk in range(13):
+                u = jnp.broadcast_to(ug_ref[kk * 16 + i : kk * 16 + i + 1, :], (8, 128))
+                block = a_buf[base : base + 64, kk * 128 : (kk + 1) * 128]
+                acc = acc + block.reshape(8, 8, 128) * u[None]
+            u = jnp.broadcast_to(ug_ref[13 * 16 + i : 13 * 16 + i + 1, :], (8, 128))
+            tail = a_buf[base : base + 64, 1664:1728].reshape(8, 8, 64) * u[None, :, 0:64]
+            acc = acc + jnp.concatenate([tail, jnp.zeros((8, 8, 64), F32)], axis=2)
+            y = jnp.sum(acc.reshape(64, 128), axis=1, keepdims=True)
+            part = jnp.sum((rt_ref[base : base + 64, :] * y).reshape(8, 8, 128), axis=0)
+            part = part + pltpu.roll(part, 4, 0)
+            part = part + pltpu.roll(part, 2, 0)
+            part = (part + pltpu.roll(part, 1, 0)) * pick_ref[i]
             out = part if out is None else out + part
-        return restrict_end(out)
+        turned = pltpu.roll(out, 64, 1)
+        return jnp.where(left, out, turned), jnp.where(left, turned, out)
 
     r1_copy.wait()
     own_r1 = r1_buf[pl.ds(pl.multiple_of(d * 64, 64), 64), :]
     hi, lo = pieces(own_r1.T)
+    rt_ref[:, 0:64] = own_r1.T
     wr_ref[:, 0:64] = hi
     wr_ref[:, 64:128] = lo
     wr_ref[:, 128:256] = jnp.zeros((1024, 128), BF16)
@@ -291,6 +309,7 @@
     swap3 = swap_copy(r31_buf, 1)
     swap3.start()
     hi, lo = pieces(own_r31.T)
+    rt_ref[:, 64:128] = own_r31.T
     wr_ref[:, 128:192] = hi
     wr_ref[:, 192:256] = lo
     unused, coarse = restrict(y0)
@@ -393,7 +412,7 @@
             pltpu.SMEM((16,), jnp.int32),
             pltpu.SMEM((8,), jnp.int32),
             pltpu.VMEM((1, 1024), F32),
-            pltpu.SMEM((16, 27), jnp.int32),
+            pltpu.VMEM((16, 27), jnp.int32),
             pltpu.VMEM((64, 512), F32),
             pltpu.VMEM((1024, 1728), F32),
             pltpu.VMEM((128, 1024), F32),
@@ -402,7 +421,10 @@
             pltpu.VMEM((2, 256, 1024), BF16),
             pltpu.VMEM((1024, 256), BF16),
             pltpu.VMEM((2, 8, 1024), F32),
-            pltpu.VMEM((2, 48, 8, 128), F32),
+            pltpu.VMEM((224, 128), BF16),
+            pltpu.VMEM((224, 128), F32),
+            pltpu.VMEM((1024, 128), F32),
+            pltpu.VMEM((16, 8, 128), F32),
             pltpu.VMEM((N_EX, 16, 128), F32),
             pltpu.VMEM((N_EX, len(QUAD), 16, 128), F32),
             pltpu.SemaphoreType.DMA((A_CHUNKS,)),

time: 48.7 us -> 47.1 us (0.967)
  Pallas kernels: 48 us -> 46.4 us
    pallas_call x1, Pallas kernels: 48 us -> 46.4 us  [body(): pl.pallas_call(kernel, out_shape=jax.ShapeDtypeStruct((8, 128), F32), in_...]
where the time goes in v2:
time: 47.1 us; the launch traced here: 47 us
  Pallas kernels  46.4 us (99%)
  local copies, waits for them, and re-layouts  0.6 us (1%)
    pallas_call x1, Pallas kernels, body(): pl.pallas_call(kernel, out_shape=jax.ShapeDtypeStruct((8, 128), F32), in_...  46.4 us

profile of v2, /device:TPU:1, one launch (start us, length us, event | category | flops | bytes accessed | tf_op | source)
XLA Modules:
  0.0 47.0 jit_solution(11395934833408735401)
XLA Ops:
  0.0 46.4 %shard_map.73 = f32[8,128]{1,0:T(8,128)S(1)} custom-call(s32[16]{0:T(128)} %agg1_hbm.1, s32[8]{0:T(128)} %agg2_hbm.1, f32[1,1024]{1,0:T(1,128)} %res_hbm.1, s32[16,27]{1,0:T(8,128)} %bitcast.7, f32[64,512]{1,0:T(8,128)} %r2_hbm.1, f32[64,1024]{1,0:T(8,128)} %bitcast.6, f32[1024,1728]{1,0:T(8,128)} %bitcast.5), custom_call_target="tpu_custom_call" | custom-call | flops 40000000 | bytes 7500000 | tf_op jit(solution)/shard_map/pallas_call | solution.py:406
  46.4 0.6 %copy.9 = f32[1,1024]{1,0:T(1,128)} copy(f32[1,1024]{1,0:T(1,128)S(1)} %bitcast.4) | data formatting | bytes 8192

commit v3 on v2

--- a/solution.py
+++ b/solution.py
@@ -15,6 +15,8 @@
 BF16 = jnp.bfloat16
 MESH = pl.DeviceIdType.MESH
 A_CHUNKS = 4
+SHIFT = 2
+SHIFT_FROM = 0
 PAIR = ((1, 0), (1, 1), (0, 1))
 QUAD = ((2, 0), (3, 0), (2, 1), (3, 1)) + PAIR
 N_EX = 10
@@ -53,6 +55,13 @@
     mask_ref,
     hot_ref,
     ug_ref,
+    ax_buf,
+    colsx_ref,
+    hotx_ref,
+    ugx_ref,
+    rtx_ref,
+    shift_send,
+    shift_recv,
     rt_ref,
     pick_ref,
     send_buf,
@@ -128,18 +137,21 @@
     for m in range(8):
         r2_blk[m] = r2_ref[:, m * 64 : (m + 1) * 64]
 
-    place = cols_ref[...] + 16 * (d - 1)
-    valid = (place >= 0) & (place < 32)
-    half = place % 2
-    inner = (place // 16) * 8 + (place % 16) // 2
-    even = jnp.where(valid, half * 16 + inner, -1)
-    odd = jnp.where(valid, 32 + (1 - half) * 16 + inner, -1)
-    spot = lax.broadcasted_iota(jnp.int32, (16, 128), 1) % 64
-    for kk in range(14):
-        hit = even[:, 2 * kk : 2 * kk + 1] == spot
-        if 2 * kk + 1 < 27:
-            hit = hit | (odd[:, 2 * kk + 1 : 2 * kk + 2] == spot)
-        hot_ref[kk * 16 : (kk + 1) * 16, :] = jnp.where(hit, 1.0, 0.0).astype(BF16)
+    def build_hot(columns, owner, target):
+        place = columns + 16 * (owner - 1)
+        valid = (place >= 0) & (place < 32)
+        half = place % 2
+        inner = (place // 16) * 8 + (place % 16) // 2
+        even = jnp.where(valid, half * 16 + inner, -1)
+        odd = jnp.where(valid, 32 + (1 - half) * 16 + inner, -1)
+        spot = lax.broadcasted_iota(jnp.int32, (16, 128), 1) % 64
+        for kk in range(14):
+            hit = even[:, 2 * kk : 2 * kk + 1] == spot
+            if 2 * kk + 1 < 27:
+                hit = hit | (odd[:, 2 * kk + 1 : 2 * kk + 2] == spot)
+            target[kk * 16 : (kk + 1) * 16, :] = jnp.where(hit, 1.0, 0.0).astype(BF16)
+
+    build_hot(cols_ref[...], d, hot_ref)
 
     def start_sends(ex, relations, rows):
         copies = []
@@ -163,9 +175,9 @@
         return jnp.where(mine, value, 0.0)
 
     def send(ex, low, high, relations):
-        send_buf[ex, 0:8] = own(low)
+        send_buf[ex, 0:8] = low
         if high is not None:
-            send_buf[ex, 8:16] = own(high)
+            send_buf[ex, 8:16] = high
         copies = start_sends(ex, relations, 8 if high is None else 16)
         started.extend(copies)
         return copies
@@ -226,7 +238,7 @@
     def own_rows(tiles):
         return jnp.where(d == 0, rows_of(tiles[0]), rows_of(tiles[1]))
 
-    def apply(v, level):
+    def apply(v, level, shifted=True):
         tiles = prolong(v, level)
         u = jnp.concatenate([rows_of(tiles[0]), rows_of(tiles[1])], axis=0)
         turned = pltpu.roll(u, 64, 1)
@@ -241,26 +253,53 @@
             axis=0,
         )
         hi, lo = pieces(spread)
-        ug_ref[...] = mm(hot_ref[...], jnp.concatenate([hi, lo], axis=0))
-        out = None
-        for i in range(16):
-            base = i * 64
-            acc = jnp.zeros((8, 8, 128), F32)
-            for kk in range(13):
-                u = jnp.broadcast_to(ug_ref[kk * 16 + i : kk * 16 + i + 1, :], (8, 128))
-                block = a_buf[base : base + 64, kk * 128 : (kk + 1) * 128]
-                acc = acc + block.reshape(8, 8, 128) * u[None]
-            u = jnp.broadcast_to(ug_ref[13 * 16 + i : 13 * 16 + i + 1, :], (8, 128))
-            tail = a_buf[base : base + 64, 1664:1728].reshape(8, 8, 64) * u[None, :, 0:64]
-            acc = acc + jnp.concatenate([tail, jnp.zeros((8, 8, 64), F32)], axis=2)
-            y = jnp.sum(acc.reshape(64, 128), axis=1, keepdims=True)
-            part = jnp.sum((rt_ref[base : base + 64, :] * y).reshape(8, 8, 128), axis=0)
-            part = part + pltpu.roll(part, 4, 0)
-            part = part + pltpu.roll(part, 2, 0)
-            part = (part + pltpu.roll(part, 1, 0)) * pick_ref[i]
-            out = part if out is None else out + part
+        rhs = jnp.concatenate([hi, lo], axis=0)
+        ug_ref[...] = mm(hot_ref[...], rhs)
+
+        def blocks(numbers, a_ref, u_ref, r_ref, first):
+            out = None
+            for i in numbers:
+                base = (i - first) * 64
+                acc = jnp.zeros((8, 8, 128), F32)
+                for kk in range(13):
+                    u = jnp.broadcast_to(u_ref[kk * 16 + i : kk * 16 + i + 1, :], (8, 128))
+                    block = a_ref[base : base + 64, kk * 128 : (kk + 1) * 128]
+                    acc = acc + block.reshape(8, 8, 128) * u[None]
+                u = jnp.broadcast_to(u_ref[13 * 16 + i : 13 * 16 + i + 1, :], (8, 128))
+                tail = a_ref[base : base + 64, 1664:1728].reshape(8, 8, 64) * u[None, :, 0:64]
+                acc = acc + jnp.concatenate([tail, jnp.zeros((8, 8, 64), F32)], axis=2)
+                y = jnp.sum(acc.reshape(64, 128), axis=1, keepdims=True)
+                part = jnp.sum((r_ref[base : base + 64, :] * y).reshape(8, 8, 128), axis=0)
+                part = part + pltpu.roll(part, 4, 0)
+                part = part + pltpu.roll(part, 2, 0)
+                part = (part + pltpu.roll(part, 1, 0)) * pick_ref[i]
+                out = part if out is None else out + part
+            return out
+
+        if shifted:
+            out = blocks(range(16 - SHIFT), a_buf, ug_ref, rt_ref, 0)
+            last = range(16 - SHIFT, 16)
+
+            def both_ends():
+                ugx_ref[...] = mm(hotx_ref[...], rhs)
+                return (
+                    blocks(last, a_buf, ug_ref, rt_ref, 0),
+                    blocks(last, ax_buf, ugx_ref, rtx_ref, 16 - SHIFT),
+                )
+
+            def neither():
+                return jnp.zeros((8, 128), F32), jnp.zeros((8, 128), F32)
+
+            more, other = lax.cond(d == 1, both_ends, neither)
+            out = out + more
+        else:
+            out = blocks(range(16), a_buf, ug_ref, rt_ref, 0)
+            other = jnp.zeros((8, 128), F32)
         turned = pltpu.roll(out, 64, 1)
-        return jnp.where(left, out, turned), jnp.where(left, turned, out)
+        other_turned = pltpu.roll(other, 64, 1)
+        w = jnp.where(mine, jnp.where(left, out, turned), jnp.where(left, other, other_turned))
+        w3 = jnp.where(mine, jnp.where(left, turned, out), jnp.where(left, other_turned, other))
+        return w, w3
 
     r1_copy.wait()
     own_r1 = r1_buf[pl.ds(pl.multiple_of(d * 64, 64), 64), :]
@@ -285,10 +324,32 @@
 
     swap1 = swap_copy(r1_buf, 0)
     swap1.start()
+    cols_copy = pltpu.make_async_remote_copy(
+        src_ref=cols_ref,
+        dst_ref=colsx_ref,
+        send_sem=shift_send.at[0],
+        recv_sem=shift_recv.at[0],
+        device_id=(g, 1 - d),
+        device_id_type=MESH,
+    )
+    cols_copy.start()
 
     y0 = jnp.broadcast_to(res_ref[...], (8, 1024))
     w, unused = restrict(y0)
-    copies = send(0, w, None, PAIR)
+    copies = send(0, own(w), None, PAIR)
+
+    a_copy = pltpu.make_async_remote_copy(
+        src_ref=a_hbm.at[pl.ds(64 * (16 - SHIFT), 64 * SHIFT)],
+        dst_ref=ax_buf,
+        send_sem=shift_send.at[1],
+        recv_sem=shift_recv.at[1],
+        device_id=(g, 1 - d),
+        device_id_type=MESH,
+    )
+
+    @pl.when(d == 0)
+    def _():
+        a_copy.start()
 
     for jj in range(8):
         parts = []
@@ -313,12 +374,21 @@
     wr_ref[:, 128:192] = hi
     wr_ref[:, 192:256] = lo
     unused, coarse = restrict(y0)
+    coarse = own(coarse)
 
     swap1.wait()
     hi, lo = pieces(r1_buf[...])
     wp_ref[0, 0:128] = hi
     wp_ref[0, 128:256] = lo
 
+    cols_copy.wait()
+    build_hot(colsx_ref[...], 1 - d, hotx_ref)
+    rtx_ref[:, 0:64] = r1_buf[pl.ds(pl.multiple_of((1 - d) * 64, 64), 64), 64 * (16 - SHIFT) :].T
+    swap3.wait()
+    rtx_ref[:, 64:128] = r31_buf[pl.ds(pl.multiple_of((1 - d) * 64, 64), 64), 64 * (16 - SHIFT) :].T
+    hi, lo = pieces(r31_buf[...])
+    wp_ref[1, 0:128] = hi
+    wp_ref[1, 128:256] = lo
     for copy in a_copies:
         copy.wait()
 
@@ -343,14 +413,16 @@
     for sweep in range(S2):
         ex = 1 + sweep
         start = start + direction
-        w, w3 = apply(direction, 0)
+        if sweep == SHIFT_FROM:
+
+            @pl.when(d == 1)
+            def _():
+                a_copy.wait_recv()
+
+        w, w3 = apply(direction, 0, sweep >= SHIFT_FROM)
         coarse = coarse - w3
         if sweep == S2 - 1:
             copies = send(ex, w, coarse, QUAD)
-            swap3.wait()
-            hi, lo = pieces(r31_buf[...])
-            wp_ref[1, 0:128] = hi
-            wp_ref[1, 128:256] = lo
             wait_all(copies)
             rest = rest - total(ex, copies, QUAD, 0, PAIR)
             rhs3 = total(ex, copies, QUAD, 8, QUAD)
@@ -398,6 +470,10 @@
 
     for copy in started:
         copy.wait_send()
+
+    @pl.when(d == 0)
+    def _():
+        a_copy.wait_send()
 
 
 def body(residual, op_blocks, block_cols, restrict_one, restrict_two, agg_one, agg_two):
@@ -423,6 +499,13 @@
             pltpu.VMEM((2, 8, 1024), F32),
             pltpu.VMEM((224, 128), BF16),
             pltpu.VMEM((224, 128), F32),
+            pltpu.VMEM((64 * SHIFT, 1728), F32),
+            pltpu.VMEM((16, 27), jnp.int32),
+            pltpu.VMEM((224, 128), BF16),
+            pltpu.VMEM((224, 128), F32),
+            pltpu.VMEM((64 * SHIFT, 128), F32),
+            pltpu.SemaphoreType.DMA((2,)),
+            pltpu.SemaphoreType.DMA((2,)),
             pltpu.VMEM((1024, 128), F32),
             pltpu.VMEM((16, 8, 128), F32),
             pltpu.VMEM((N_EX, 16, 128), F32),

time: 47.1 us -> 46.3 us (0.983)
  Pallas kernels: 46.4 us -> 45.6 us
    pallas_call x1, Pallas kernels: 46.4 us -> 45.6 us  [body(): pl.pallas_call(kernel, out_shape=jax.ShapeDtypeStruct((8, 128), F32), in_...]
where the time goes in v3:
time: 46.3 us; the launch traced here: 46.2 us
  Pallas kernels  45.6 us (98%)
  local copies, waits for them, and re-layouts  0.6 us (1%)
    pallas_call x1, Pallas kernels, body(): pl.pallas_call(kernel, out_shape=jax.ShapeDtypeStruct((8, 128), F32), in_...  45.6 us

profile of v3, /device:TPU:1, one launch (start us, length us, event | category | flops | bytes accessed | tf_op | source)
XLA Modules:
  0.0 46.2 jit_solution(12087296120672738008)
XLA Ops:
  0.0 45.6 %shard_map.73 = f32[8,128]{1,0:T(8,128)S(1)} custom-call(s32[16]{0:T(128)} %agg1_hbm.1, s32[8]{0:T(128)} %agg2_hbm.1, f32[1,1024]{1,0:T(1,128)} %res_hbm.1, s32[16,27]{1,0:T(8,128)} %bitcast.7, f32[64,512]{1,0:T(8,128)} %r2_hbm.1, f32[64,1024]{1,0:T(8,128)} %bitcast.6, f32[1024,1728]{1,0:T(8,128)} %bitcast.5), custom_call_target="tpu_custom_call" | custom-call | flops 40000000 | bytes 7500000 | tf_op jit(solution)/shard_map/pallas_call | solution.py:482
  45.7 0.6 %copy.9 = f32[1,1024]{1,0:T(1,128)} copy(f32[1,1024]{1,0:T(1,128)S(1)} %bitcast.4) | data formatting | bytes 8192

commit v4 on v3

--- a/solution.py
+++ b/solution.py
@@ -86,6 +86,10 @@
             chip = chip + 2 - 4 * ((g // 2) % 2)
         return (chip, 1 - d if core else d)
 
+    barrier = pltpu.get_barrier_semaphore()
+    for relation in QUAD:
+        pl.semaphore_signal(barrier, inc=1, device_id=peer(relation), device_id_type=MESH)
+
     r1_copy = pltpu.make_async_copy(r1_hbm, r1_buf.at[pl.ds(d * 64, 64)], r1_sem)
     r1_copy.start()
     inputs = []
@@ -93,8 +97,8 @@
         (
             (agg1_hbm, agg1_ref),
             (agg2_hbm, agg2_ref),
+            (res_hbm, res_ref),
             (cols_hbm, cols_ref),
-            (res_hbm, res_ref),
             (r2_hbm, r2_ref),
         )
     ):
@@ -107,16 +111,12 @@
         a_copies.append(pltpu.make_async_copy(a_hbm.at[cut], a_buf.at[cut], a_sem.at[part]))
         a_copies[-1].start()
 
-    barrier = pltpu.get_barrier_semaphore()
-    for relation in QUAD:
-        pl.semaphore_signal(barrier, inc=1, device_id=peer(relation), device_id_type=MESH)
-
     lane = lax.broadcasted_iota(jnp.int32, (8, 128), 1)
     row = lax.broadcasted_iota(jnp.int32, (8, 128), 0)
     left = lane < 64
     mine = (lane // 64) == d
 
-    for copy in inputs:
+    for copy in inputs[0:3]:
         copy.wait()
 
     aggs = []
@@ -130,12 +130,6 @@
         cut = slice(jj * 128, (jj + 1) * 128)
         mask_ref[0, :, cut] = jnp.where(m1, 1.0, 0.0).astype(F32)
         mask_ref[1, :, cut] = jnp.where(m3, 1.0, 0.0).astype(F32)
-
-    for j in range(16):
-        pick_ref[j] = jnp.where(jnp.where(left, aggs[j], agg2_ref[aggs[j]] // 2) == row, 1.0, 0.0)
-
-    for m in range(8):
-        r2_blk[m] = r2_ref[:, m * 64 : (m + 1) * 64]
 
     def build_hot(columns, owner, target):
         place = columns + 16 * (owner - 1)
@@ -150,8 +144,6 @@
             if 2 * kk + 1 < 27:
                 hit = hit | (odd[:, 2 * kk + 1 : 2 * kk + 2] == spot)
             target[kk * 16 : (kk + 1) * 16, :] = jnp.where(hit, 1.0, 0.0).astype(BF16)
-
-    build_hot(cols_ref[...], d, hot_ref)
 
     def start_sends(ex, relations, rows):
         copies = []
@@ -174,19 +166,20 @@
     def own(value):
         return jnp.where(mine, value, 0.0)
 
-    def send(ex, low, high, relations):
+    def send(ex, low, high, relations, rows=8):
         send_buf[ex, 0:8] = low
         if high is not None:
             send_buf[ex, 8:16] = high
-        copies = start_sends(ex, relations, 8 if high is None else 16)
+        copies = start_sends(ex, relations, rows)
         started.extend(copies)
         return copies
 
-    def total(ex, copies, relations, base, relations_used):
-        slots = [QUAD.index(relation) for relation in relations_used]
-        value = send_buf[ex, base : base + 8]
-        for slot in slots:
-            value = value + recv_buf[ex, slot, base : base + 8]
+    def total(ex, relations, base, rows):
+        value = send_buf[ex, base : base + rows]
+        for relation in relations:
+            value = value + recv_buf[ex, QUAD.index(relation), base : base + rows]
+        if rows < 8:
+            value = jnp.concatenate([value, jnp.zeros((8 - rows, 128), F32)], axis=0)
         return value
 
     def restrict_part(y, group, rows):
@@ -304,10 +297,8 @@
     r1_copy.wait()
     own_r1 = r1_buf[pl.ds(pl.multiple_of(d * 64, 64), 64), :]
     hi, lo = pieces(own_r1.T)
-    rt_ref[:, 0:64] = own_r1.T
     wr_ref[:, 0:64] = hi
     wr_ref[:, 64:128] = lo
-    wr_ref[:, 128:256] = jnp.zeros((1024, 128), BF16)
 
     pl.semaphore_wait(barrier, len(QUAD))
 
@@ -324,6 +315,15 @@
 
     swap1 = swap_copy(r1_buf, 0)
     swap1.start()
+    y0 = jnp.broadcast_to(res_ref[...], (8, 1024))
+    hi, lo = pieces(y0 * mask_ref[0])
+    w = mm(jnp.concatenate([hi, lo], axis=0), wr_ref[:, 0:128])
+    w = w[0:8] + w[8:16]
+    w = w + pltpu.roll(w, 64, 1)
+    copies = send(0, own(w), None, PAIR)
+
+    for copy in inputs[3:5]:
+        copy.wait()
     cols_copy = pltpu.make_async_remote_copy(
         src_ref=cols_ref,
         dst_ref=colsx_ref,
@@ -334,10 +334,6 @@
     )
     cols_copy.start()
 
-    y0 = jnp.broadcast_to(res_ref[...], (8, 1024))
-    w, unused = restrict(y0)
-    copies = send(0, own(w), None, PAIR)
-
     a_copy = pltpu.make_async_remote_copy(
         src_ref=a_hbm.at[pl.ds(64 * (16 - SHIFT), 64 * SHIFT)],
         dst_ref=ax_buf,
@@ -350,6 +346,9 @@
     @pl.when(d == 0)
     def _():
         a_copy.start()
+
+    for m in range(8):
+        r2_blk[m] = r2_ref[:, m * 64 : (m + 1) * 64]
 
     for jj in range(8):
         parts = []
@@ -381,14 +380,16 @@
     wp_ref[0, 0:128] = hi
     wp_ref[0, 128:256] = lo
 
+    for j in range(16):
+        pick_ref[j] = jnp.where(jnp.where(left, aggs[j], agg2_ref[aggs[j]] // 2) == row, 1.0, 0.0)
+
+    rt_ref[:, 0:64] = own_r1.T
+    build_hot(cols_ref[...], d, hot_ref)
     cols_copy.wait()
     build_hot(colsx_ref[...], 1 - d, hotx_ref)
     rtx_ref[:, 0:64] = r1_buf[pl.ds(pl.multiple_of((1 - d) * 64, 64), 64), 64 * (16 - SHIFT) :].T
     swap3.wait()
     rtx_ref[:, 64:128] = r31_buf[pl.ds(pl.multiple_of((1 - d) * 64, 64), 64), 64 * (16 - SHIFT) :].T
-    hi, lo = pieces(r31_buf[...])
-    wp_ref[1, 0:128] = hi
-    wp_ref[1, 128:256] = lo
     for copy in a_copies:
         copy.wait()
 
@@ -400,11 +401,11 @@
 
     def pair_total(ex, copies):
         wait_all(copies)
-        return total(ex, copies, PAIR, 0, PAIR)
-
-    def quad_total(ex, copies, base=0):
+        return total(ex, PAIR, 0, 8)
+
+    def quad_total(ex, copies):
         wait_all(copies)
-        return total(ex, copies, QUAD, base, QUAD)
+        return total(ex, QUAD, 0, 4)
 
     rest = pair_total(0, copies)
     start = jnp.zeros((8, 128), F32)
@@ -422,12 +423,16 @@
         w, w3 = apply(direction, 0, sweep >= SHIFT_FROM)
         coarse = coarse - w3
         if sweep == S2 - 1:
-            copies = send(ex, w, coarse, QUAD)
+            copies = send(ex, w, coarse, QUAD, 12)
             wait_all(copies)
-            rest = rest - total(ex, copies, QUAD, 0, PAIR)
-            rhs3 = total(ex, copies, QUAD, 8, QUAD)
+            rest = rest - total(ex, PAIR, 0, 8)
+            rhs3 = total(ex, QUAD, 8, 4)
         else:
             copies = send(ex, w, None, PAIR)
+            if sweep == 0:
+                hi, lo = pieces(r31_buf[...])
+                wp_ref[1, 0:128] = hi
+                wp_ref[1, 128:256] = lo
             rest = rest - pair_total(ex, copies)
             ratio_next = 1.0 / (2.0 * spread_ratio - ratio)
             direction = ratio_next * ratio * direction + 2.0 * ratio_next / HALF_WIDTH * rest
@@ -442,7 +447,7 @@
         if sweep < S3 - 1:
             ex = 1 + S2 + sweep
             unused, w3 = apply(direction, 1)
-            copies = send(ex, w3, None, QUAD)
+            copies = send(ex, w3, None, QUAD, 4)
             rest3 = rest3 - quad_total(ex, copies)
             ratio_next = 1.0 / (2.0 * spread_ratio - ratio)
             direction = ratio_next * ratio * direction + 2.0 * ratio_next / HALF_WIDTH * rest3

time: 46.3 us -> 45.9 us (level)
  no operation moved by 1% of the time
where the time goes in v4:
time: 45.9 us; the launch traced here: 45.8 us
  Pallas kernels  45.2 us (98%)
  local copies, waits for them, and re-layouts  0.6 us (1%)
    pallas_call x1, Pallas kernels, body(): pl.pallas_call(kernel, out_shape=jax.ShapeDtypeStruct((8, 128), F32), in_...  45.2 us

profile of v4, /device:TPU:1, one launch (start us, length us, event | category | flops | bytes accessed | tf_op | source)
XLA Modules:
  0.0 45.8 jit_solution(15099513121219669841)
XLA Ops:
  0.0 45.2 %shard_map.73 = f32[8,128]{1,0:T(8,128)S(1)} custom-call(s32[16]{0:T(128)} %agg1_hbm.1, s32[8]{0:T(128)} %agg2_hbm.1, f32[1,1024]{1,0:T(1,128)} %res_hbm.1, s32[16,27]{1,0:T(8,128)} %bitcast.7, f32[64,512]{1,0:T(8,128)} %r2_hbm.1, f32[64,1024]{1,0:T(8,128)} %bitcast.6, f32[1024,1728]{1,0:T(8,128)} %bitcast.5), custom_call_target="tpu_custom_call" | custom-call | flops 40000000 | bytes 7500000 | tf_op jit(solution)/shard_map/pallas_call | solution.py:487
  45.2 0.6 %copy.9 = f32[1,1024]{1,0:T(1,128)} copy(f32[1,1024]{1,0:T(1,128)S(1)} %bitcast.4) | data formatting | bytes 8192

commit v5 on v4

--- a/solution.py
+++ b/solution.py
@@ -14,7 +14,7 @@
 F32 = jnp.float32
 BF16 = jnp.bfloat16
 MESH = pl.DeviceIdType.MESH
-A_CHUNKS = 4
+A_CHUNKS = 1
 SHIFT = 2
 SHIFT_FROM = 0
 PAIR = ((1, 0), (1, 1), (0, 1))

time: 45.9 us -> 45.1 us (0.983)
  Pallas kernels: 45.2 us -> 44.4 us
    pallas_call x1, Pallas kernels: 45.2 us -> 44.4 us  [body(): pl.pallas_call(kernel, out_shape=jax.ShapeDtypeStruct((8, 128), F32), in_...]
where the time goes in v5:
time: 45.1 us; the launch traced here: 45 us
  Pallas kernels  44.4 us (98%)
  local copies, waits for them, and re-layouts  0.6 us (1%)
    pallas_call x1, Pallas kernels, body(): pl.pallas_call(kernel, out_shape=jax.ShapeDtypeStruct((8, 128), F32), in_...  44.4 us

profile of v5, /device:TPU:1, one launch (start us, length us, event | category | flops | bytes accessed | tf_op | source)
XLA Modules:
  0.0 45.0 jit_solution(494090303636429831)
XLA Ops:
  0.0 44.4 %shard_map.73 = f32[8,128]{1,0:T(8,128)S(1)} custom-call(s32[16]{0:T(128)} %agg1_hbm.1, s32[8]{0:T(128)} %agg2_hbm.1, f32[1,1024]{1,0:T(1,128)} %res_hbm.1, s32[16,27]{1,0:T(8,128)} %bitcast.7, f32[64,512]{1,0:T(8,128)} %r2_hbm.1, f32[64,1024]{1,0:T(8,128)} %bitcast.6, f32[1024,1728]{1,0:T(8,128)} %bitcast.5), custom_call_target="tpu_custom_call" | custom-call | flops 40000000 | bytes 7500000 | tf_op jit(solution)/shard_map/pallas_call | solution.py:487
  44.4 0.6 %copy.9 = f32[1,1024]{1,0:T(1,128)} copy(f32[1,1024]{1,0:T(1,128)S(1)} %bitcast.4) | data formatting | bytes 8192
